TPU v7x, 32 devices: a whole 2x2x4 slice. The times are simulated.
32 devices in a mesh: dp: 2 (over core), expert: 16 (over z, y, x).
Axes of the slice: x: 2, y: 2, z: 4, core: 2. Of those that a mesh axis runs over, the one named last changes fastest.
Arguments:
- states: bfloat16 [3, 4096, 1024], P(None, ('dp', 'expert')), may hold values from -6 to 6
- language: int32 [3, 4096, 1], P(None, ('dp', 'expert')), may hold values from 0 to 15; in each aligned block of 128 rows (0 to 127, 128 to 255, ..., all dimensions but the last counted through in order) at most 16 rows name the same one
- placement: int32 [3, 16], replicated, may hold values from 0 to 15, each once within a row
- swap_flags: int32 [16], replicated, may hold values from 0 to 1, as said below
- up_weight: bfloat16 [16, 1024, 4096], P('expert', None, 'dp'), may hold values from -0.1875 to 0.1875
- down_weight: bfloat16 [16, 4096, 1024], P('expert', 'dp'), may hold values from -0.09375 to 0.09375
Outputs:
- updated: bfloat16 [3, 4096, 1024], P(None, ('dp', 'expert'))
Inputs may be any that keep to these rules, and one draw needn't show every extreme that they name: In the 128 rows of one device at one step (aligned blocks along the rows), no language id occurs more than 16 times, and some id occurs exactly 16 times. `placement`: each step's row is a permutation of the devices of the expert axis. swap_flags[j] equals swap_flags[j + 8] for j under 16/2.
All inputs are finite; a program needn't handle non-finite values.
Results may differ from a plain program's by a relative error of at most 0.0047.
Values may be sent and summed in bfloat16 or wider, within the bound.
A program may use at most 128 MiB of HBM per device.

v0:
```python
import jax
import jax.numpy as jnp
from jax import lax
from jax.sharding import PartitionSpec as P


def shifted(value, axis, by):
    devices = lax.axis_size(axis)
    return lax.ppermute(value, axis, [(i, (i + by) % devices) for i in range(devices)])


def make_expert(up_matrix, down_matrix):

    def apply_rows(shard_rows):
        hidden = jnp.maximum(
            jnp.dot(shard_rows, up_matrix, preferred_element_type=jnp.float32), 0.0
        ).astype(jnp.bfloat16)
        return jnp.dot(hidden, down_matrix, preferred_element_type=jnp.float32)

    def expert_fn(arrived):
        source_count, slot_count, model_width = arrived.shape
        flat_rows = arrived.reshape(source_count * slot_count, model_width)
        partial_terms = apply_rows(lax.all_gather(flat_rows, "dp", axis=0, tiled=True))
        own_share = lax.psum_scatter(partial_terms, "dp", scatter_dimension=0, tiled=True)
        return own_share.astype(jnp.bfloat16).reshape(source_count, slot_count, model_width)

    return expert_fn


def shards(states, language, placement, swap_flags, up_weight, down_weight):
    step_count, row_count, model_width = states.shape
    experts = lax.axis_size("expert")
    capacity = max(2, 2 * row_count // experts)
    labels = jnp.arange(experts, dtype=jnp.int32)
    up_local = up_weight[0]
    down_local = down_weight[0]
    own_flag = jnp.sum(jnp.where(labels == lax.axis_index("expert"), swap_flags, 0))
    partner_up, partner_down = shifted((up_local, down_local), "expert", experts // 2)
    later_up = jnp.where(own_flag == 1, partner_up, up_local)
    later_down = jnp.where(own_flag == 1, partner_down, down_local)
    slot_labels = jnp.arange(experts * capacity, dtype=jnp.int32)
    outputs = []
    for step_index in range(step_count):
        lang_hot = (language[step_index, :, 0][:, None] == labels[None, :]).astype(jnp.int32)
        target = jnp.sum(lang_hot * placement[step_index][None, :], axis=1)
        dest_hot = (target[:, None] == labels[None, :]).astype(jnp.int32)
        earlier = jnp.cumsum(dest_hot, axis=0) - dest_hot
        position_in = jnp.sum(earlier * dest_hot, axis=1)
        slot_index = target * capacity + position_in
        select = (slot_index[:, None] == slot_labels[None, :]).astype(jnp.bfloat16)
        outgoing = jnp.einsum(
            "rs,rd->sd", select, states[step_index], preferred_element_type=jnp.float32
        )
        outgoing = outgoing.astype(jnp.bfloat16).reshape(experts, capacity, model_width)
        if step_index == 0:
            expert_fn = make_expert(up_local, down_local)
        else:
            expert_fn = make_expert(later_up, later_down)
        served = expert_fn(
            lax.all_to_all(outgoing, "expert", split_axis=0, concat_axis=0, tiled=True)
        )
        returned = lax.all_to_all(served, "expert", split_axis=0, concat_axis=0, tiled=True)
        selected = jnp.dot(
            select,
            returned.reshape(experts * capacity, model_width),
            preferred_element_type=jnp.float32,
        )
        outputs.append((states[step_index].astype(jnp.float32) + selected).astype(jnp.bfloat16))
    return jnp.stack(outputs)


def solution(mesh):
    placed = (
        P(None, ("dp", "expert"), None),
        P(None, ("dp", "expert"), None),
        P(),
        P(),
        P("expert", None, "dp"),
        P("expert", "dp", None),
    )
    return jax.shard_map(
        shards,
        mesh=mesh,
        in_specs=placed,
        out_specs=P(None, ("dp", "expert"), None),
        check_vma=False,
    )
```

profile of v0, /device:TPU:15, one launch (start us, length us, event | category | flops | bytes accessed | tf_op | source)
XLA Modules:
  0.0 520.0 jit_solution(7745899966715773895)
XLA Ops:
  6.5 0.8 slice_bitcast_fusion.5
  7.3 0.8 slice_bitcast_fusion.4
  8.1 0.2 select_reduce_fusion.5
  8.3 0.1 fusion.23
  8.4 0.2 reduce_window_sum.20
  8.5 0.2 select_reduce_fusion.4
  8.7 2.2 convolution_convert_fusion.2
  10.9 6.6 %all-to-all-start = ((bf16[16,16,1024]{2,1,0:T(8,128)(2,1)}), bf16[16,16,1024]{2,1,0:T(8,128)(2,1)S(1)}, u32[]{:S(2)}, u32[]{:S(2)}) async-start(bf16[16,16,1024]{2,1,0:T(8,128)(2,1)} %bitcast.3), calls=%async_computation | async-start | bytes 1048576 | tf_op jit(solution)/shard_map/all_to_all | solution.py:60
  17.5 0.0 all-gather.4.cloned.1.call-start
  17.5 0.2 select_reduce_fusion.1
  17.7 0.1 fusion.20
  17.8 0.2 reduce_window_sum.24
  18.0 0.2 select_reduce_fusion.2
  18.1 11.8 %all-to-all-done = bf16[16,16,1024]{2,1,0:T(8,128)(2,1)S(1)} async-done(((bf16[16,16,1024]{2,1,0:T(8,128)(2,1)}), bf16[16,16,1024]{2,1,0:T(8,128)(2,1)S(1)}, u32[]{:S(2)}, u32[]{:S(2)}) %all-to-all-start) | async-done | bytes 524320 | tf_op jit(solution)/shard_map/all_to_all | solution.py:60
  30.0 0.8 copy-done.1
  30.8 0.0 all-gather.4.cloned.1.call-update
  30.8 2.2 convolution_convert_fusion.1
  33.0 5.8 %all-to-all-start.2 = ((bf16[16,16,1024]{2,1,0:T(8,128)(2,1)}), bf16[16,16,1024]{2,1,0:T(8,128)(2,1)S(1)}, u32[]{:S(2)}, u32[]{:S(2)}) async-start(bf16[16,16,1024]{2,1,0:T(8,128)(2,1)} %bitcast.13), calls=%async_computation.3 | async-start | bytes 1048576 | tf_op jit(solution)/shard_map/all_to_all | solution.py:60
  38.7 0.0 all-gather.6.cloned.1.call-start
  38.8 0.1 fusion.17
  38.9 0.2 reduce_window_sum.25
  39.0 0.2 select_reduce_fusion
  39.2 12.0 %all-to-all-done.2 = bf16[16,16,1024]{2,1,0:T(8,128)(2,1)S(1)} async-done(((bf16[16,16,1024]{2,1,0:T(8,128)(2,1)}), bf16[16,16,1024]{2,1,0:T(8,128)(2,1)S(1)}, u32[]{:S(2)}, u32[]{:S(2)}) %all-to-all-start.2) | async-done | bytes 524320 | tf_op jit(solution)/shard_map/all_to_all | solution.py:60
  51.2 0.8 copy-done.2
  52.1 0.0 all-gather.6.cloned.1.call-update
  52.1 1.2 convolution_convert_fusion
  53.3 5.7 %all-to-all-start.4 = ((bf16[16,16,1024]{2,1,0:T(8,128)(2,1)}), bf16[16,16,1024]{2,1,0:T(8,128)(2,1)S(1)}, u32[]{:S(2)}, u32[]{:S(2)}) async-start(bf16[16,16,1024]{2,1,0:T(8,128)(2,1)} %bitcast.21), calls=%async_computation.6 | async-start | bytes 1048576 | tf_op jit(solution)/shard_map/all_to_all | solution.py:60
  59.0 0.0 all-gather.8.cloned.1.call-start
  59.0 2.2 collective-permute-start
  61.2 0.3 collective-permute-start.1
  61.5 189.8 %all-to-all-done.4 = bf16[16,16,1024]{2,1,0:T(8,128)(2,1)S(1)} async-done(((bf16[16,16,1024]{2,1,0:T(8,128)(2,1)}), bf16[16,16,1024]{2,1,0:T(8,128)(2,1)S(1)}, u32[]{:S(2)}, u32[]{:S(2)}) %all-to-all-start.4) | async-done | bytes 524320 | tf_op jit(solution)/shard_map/all_to_all | solution.py:60
  251.3 0.8 copy-done.3
  252.0 0.0 all-gather.8.cloned.1.call-update
  252.1 0.0 reduce-scatter.4.cloned.1.call-start
  252.1 0.0 all-gather.4.cloned.1.call-done
  252.2 9.7 %fusion.8 = f32[512,1024]{1,0:T(8,128)} fusion(bf16[512,1024]{1,0:T(8,128)(2,1)} %all-gather.4.cloned.1.call-done, bf16[1,2048,1024]{2,1,0:T(8,128)(2,1)} %param.11, bf16[1,1024,2048]{2,1,0:T(8,128)(2,1)} %param.10), kind=kOutput, calls=%fused_computation.19 | convolution fusion | flops 4297064448 | bytes 11534336 | tf_op jit(solution)/shard_map/dot_general | solution.py:18
  261.8 0.0 reduce-scatter.4.cloned.1.call-update
  261.8 0.0 reduce-scatter.6.cloned.1.call-start
  261.9 0.7 fusion.24
  263.2 0.0 all-gather.6.cloned.1.call-done
  263.2 76.6 %collective-permute-done = bf16[1024,2048]{1,0:T(8,128)(2,1)} collective-permute-done((bf16[1024,2048]{1,0:T(8,128)(2,1)}, bf16[1024,2048]{1,0:T(8,128)(2,1)}, u32[]{:S(2)}, u32[]{:S(2)}) %collective-permute-start) | collective-permute-done | bytes 4194336 | tf_op jit(solution)/shard_map/ppermute | solution.py:9
  339.8 89.9 %collective-permute-done.1 = bf16[2048,1024]{1,0:T(8,128)(2,1)} collective-permute-done((bf16[2048,1024]{1,0:T(8,128)(2,1)}, bf16[2048,1024]{1,0:T(8,128)(2,1)}, u32[]{:S(2)}, u32[]{:S(2)}) %collective-permute-start.1) | collective-permute-done | bytes 4194336 | tf_op jit(solution)/shard_map/ppermute | solution.py:9
  429.7 9.6 %fusion.1 = f32[512,1024]{1,0:T(8,128)} fusion(bf16[2048,1024]{1,0:T(8,128)(2,1)} %collective-permute-done.1, pred[]{:T(512)S(6)} %eq.155, bf16[512,1024]{1,0:T(8,128)(2,1)} %all-gather.6.cloned.1.call-done, bf16[1024,2048]{1,0:T(8,128)(2,1)} %collective-permute-done, bf16[1,2048,1024]{2,1,0:T(8,128)(2,1)} %param.11, bf16[1,1024,2048]{2,1,0:T(8,128)(2,1)} %param.10), kind=kOutput, calls=%fused_computation.6 | convolution fusion | flops 4301258752 | bytes 19922944 | tf_op jit(solution)/shard_map/dot_general | solution.py:18
  439.3 0.0 reduce-scatter.6.cloned.1.call-update
  439.4 0.2 reduce-scatter.8.cloned.1.call-start
  439.6 0.0 all-gather.8.cloned.1.call-done
  439.6 9.6 %fusion = f32[512,1024]{1,0:T(8,128)} fusion(bf16[2048,1024]{1,0:T(8,128)(2,1)} %collective-permute-done.1, pred[]{:T(512)S(6)} %eq.155, bf16[512,1024]{1,0:T(8,128)(2,1)} %all-gather.8.cloned.1.call-done, bf16[1024,2048]{1,0:T(8,128)(2,1)} %collective-permute-done, bf16[1,2048,1024]{2,1,0:T(8,128)(2,1)} %param.11, bf16[1,1024,2048]{2,1,0:T(8,128)(2,1)} %param.10), kind=kOutput, calls=%fused_computation.5 | convolution fusion | flops 4301258752 | bytes 19922944 | tf_op jit(solution)/shard_map/dot_general | solution.py:18
  449.2 0.0 reduce-scatter.8.cloned.1.call-update
  449.2 0.0 reduce-scatter.4.cloned.1.call-done
  449.3 2.4 convert_element_type.64
  451.7 11.4 %all-to-all-start.1 = ((bf16[16,16,1024]{2,1,0:T(8,128)(2,1)}), bf16[16,16,1024]{2,1,0:T(8,128)(2,1)S(1)}, u32[]{:S(2)}, u32[]{:S(2)}) async-start(bf16[16,16,1024]{2,1,0:T(8,128)(2,1)} %bitcast.7), calls=%async_computation.2 | async-start | bytes 1048576 | tf_op jit(solution)/shard_map/all_to_all | solution.py:62
  463.1 0.0 reduce-scatter.6.cloned.1.call-done
  463.1 2.1 convert_element_type.70
  465.3 10.4 %all-to-all-done.1 = bf16[16,16,1024]{2,1,0:T(8,128)(2,1)S(1)} async-done(((bf16[16,16,1024]{2,1,0:T(8,128)(2,1)}), bf16[16,16,1024]{2,1,0:T(8,128)(2,1)S(1)}, u32[]{:S(2)}, u32[]{:S(2)}) %all-to-all-start.1) | async-done | bytes 524320 | tf_op jit(solution)/shard_map/all_to_all | solution.py:62
  475.6 5.7 %all-to-all-start.3 = ((bf16[16,16,1024]{2,1,0:T(8,128)(2,1)}), bf16[16,16,1024]{2,1,0:T(8,128)(2,1)S(1)}, u32[]{:S(2)}, u32[]{:S(2)}) async-start(bf16[16,16,1024]{2,1,0:T(8,128)(2,1)} %bitcast.15), calls=%async_computation.5 | async-start | bytes 1048576 | tf_op jit(solution)/shard_map/all_to_all | solution.py:62
  481.3 0.0 reduce-scatter.8.cloned.1.call-done
  481.3 2.1 convert_element_type.76
  483.4 10.4 %all-to-all-done.3 = bf16[16,16,1024]{2,1,0:T(8,128)(2,1)S(1)} async-done(((bf16[16,16,1024]{2,1,0:T(8,128)(2,1)}), bf16[16,16,1024]{2,1,0:T(8,128)(2,1)S(1)}, u32[]{:S(2)}, u32[]{:S(2)}) %all-to-all-start.3) | async-done | bytes 524320 | tf_op jit(solution)/shard_map/all_to_all | solution.py:62
  493.8 5.6 %all-to-all-start.5 = ((bf16[16,16,1024]{2,1,0:T(8,128)(2,1)}), bf16[16,16,1024]{2,1,0:T(8,128)(2,1)S(1)}, u32[]{:S(2)}, u32[]{:S(2)}) async-start(bf16[16,16,1024]{2,1,0:T(8,128)(2,1)} %bitcast.23), calls=%async_computation.8 | async-start | bytes 1048576 | tf_op jit(solution)/shard_map/all_to_all | solution.py:62
  499.4 0.3 fusion.7
  499.6 0.3 fusion.6
  499.9 12.0 %all-to-all-done.5 = bf16[16,16,1024]{2,1,0:T(8,128)(2,1)S(1)} async-done(((bf16[16,16,1024]{2,1,0:T(8,128)(2,1)}), bf16[16,16,1024]{2,1,0:T(8,128)(2,1)S(1)}, u32[]{:S(2)}, u32[]{:S(2)}) %all-to-all-start.5) | async-done | bytes 524320 | tf_op jit(solution)/shard_map/all_to_all | solution.py:62
  511.9 0.3 fusion.5
  512.2 1.0 pad_maximum_fusion
  (10 shorter events, 0.0 us)
Async XLA Ops:
  6.5 45.6 %copy-start = (bf16[3,128,1024]{2,1,0:T(8,128)(2,1)S(1)}, bf16[3,128,1024]{2,1,0:T(8,128)(2,1)}, u32[]{:S(2)}) copy-start(bf16[3,128,1024]{2,1,0:T(8,128)(2,1)} %param.6) | copy-start | bytes 2359300
  10.9 19.1 %all-to-all-start = ((bf16[16,16,1024]{2,1,0:T(8,128)(2,1)}), bf16[16,16,1024]{2,1,0:T(8,128)(2,1)S(1)}, u32[]{:S(2)}, u32[]{:S(2)}) async-start(bf16[16,16,1024]{2,1,0:T(8,128)(2,1)} %bitcast.3), calls=%async_computation | async-start | bytes 1048576 | tf_op jit(solution)/shard_map/all_to_all | solution.py:60
  17.5 234.7 %all-gather.4.cloned.1.call-start = ((), (), s32[]{:S(2)}) async-start(), calls=%async_computation.9 | async-start | bytes 1572864 | tf_op jit(solution)/shard_map/all_gather | solution.py:23
  30.0 0.8 copy-start.1
  33.0 18.3 %all-to-all-start.2 = ((bf16[16,16,1024]{2,1,0:T(8,128)(2,1)}), bf16[16,16,1024]{2,1,0:T(8,128)(2,1)S(1)}, u32[]{:S(2)}, u32[]{:S(2)}) async-start(bf16[16,16,1024]{2,1,0:T(8,128)(2,1)} %bitcast.13), calls=%async_computation.3 | async-start | bytes 1048576 | tf_op jit(solution)/shard_map/all_to_all | solution.py:60
  38.7 224.5 %all-gather.6.cloned.1.call-start = ((), (), s32[]{:S(2)}) async-start(), calls=%async_computation.11 | async-start | bytes 1572864 | tf_op jit(solution)/shard_map/all_gather | solution.py:23
  51.2 0.8 copy-start.2
  53.3 197.9 %all-to-all-start.4 = ((bf16[16,16,1024]{2,1,0:T(8,128)(2,1)}), bf16[16,16,1024]{2,1,0:T(8,128)(2,1)S(1)}, u32[]{:S(2)}, u32[]{:S(2)}) async-start(bf16[16,16,1024]{2,1,0:T(8,128)(2,1)} %bitcast.21), calls=%async_computation.6 | async-start | bytes 1048576 | tf_op jit(solution)/shard_map/all_to_all | solution.py:60
  59.0 380.6 %all-gather.8.cloned.1.call-start = ((), (), s32[]{:S(2)}) async-start(), calls=%async_computation.13 | async-start | bytes 1572864 | tf_op jit(solution)/shard_map/all_gather | solution.py:23
  59.0 280.8 %collective-permute-start = (bf16[1024,2048]{1,0:T(8,128)(2,1)}, bf16[1024,2048]{1,0:T(8,128)(2,1)}, u32[]{:S(2)}, u32[]{:S(2)}) collective-permute-start(bf16[1024,2048]{1,0:T(8,128)(2,1)} %bitcast.80), channel_id=1, source_target_pairs={{0,8},{1,9},{2,10},{3,11},{4,12},{5,13},{6,14},{7,15},{8,0},{9,1},... | collective-permute-start | bytes 12582920 | tf_op jit(solution)/shard_map/ppermute | solution.py:9
  61.2 368.5 %collective-permute-start.1 = (bf16[2048,1024]{1,0:T(8,128)(2,1)}, bf16[2048,1024]{1,0:T(8,128)(2,1)}, u32[]{:S(2)}, u32[]{:S(2)}) collective-permute-start(bf16[2048,1024]{1,0:T(8,128)(2,1)} %bitcast.79), channel_id=1, source_target_pairs={{0,8},{1,9},{2,10},{3,11},{4,12},{5,13},{6,14},{7,15},{8,0},{9,1},... | collective-permute-start | bytes 12582920 | tf_op jit(solution)/shard_map/ppermute | solution.py:9
  251.3 0.8 copy-start.3
  252.1 9.8 %copy-start.4 = (s32[16]{0:T(128)S(1)}, s32[16]{0:T(128)}, u32[]{:S(2)}) copy-start(s32[16]{0:T(128)} %param.9) | copy-start | bytes 196
  252.1 197.2 %reduce-scatter.4.cloned.1.call-start = ((), (), s32[]{:S(2)}) async-start(), calls=%async_computation.10 | async-start | bytes 3145728 | tf_op jit(solution)/shard_map/reduce_scatter | solution.py:24
  261.8 201.3 %reduce-scatter.6.cloned.1.call-start = ((), (), s32[]{:S(2)}) async-start(), calls=%async_computation.12 | async-start | bytes 3145728 | tf_op jit(solution)/shard_map/reduce_scatter | solution.py:24
  439.4 41.9 %reduce-scatter.8.cloned.1.call-start = ((), (), s32[]{:S(2)}) async-start(), calls=%async_computation.14 | async-start | bytes 3145728 | tf_op jit(solution)/shard_map/reduce_scatter | solution.py:24
  451.7 24.0 %all-to-all-start.1 = ((bf16[16,16,1024]{2,1,0:T(8,128)(2,1)}), bf16[16,16,1024]{2,1,0:T(8,128)(2,1)S(1)}, u32[]{:S(2)}, u32[]{:S(2)}) async-start(bf16[16,16,1024]{2,1,0:T(8,128)(2,1)} %bitcast.7), calls=%async_computation.2 | async-start | bytes 1048576 | tf_op jit(solution)/shard_map/all_to_all | solution.py:62
  475.6 18.2 %all-to-all-start.3 = ((bf16[16,16,1024]{2,1,0:T(8,128)(2,1)}), bf16[16,16,1024]{2,1,0:T(8,128)(2,1)S(1)}, u32[]{:S(2)}, u32[]{:S(2)}) async-start(bf16[16,16,1024]{2,1,0:T(8,128)(2,1)} %bitcast.15), calls=%async_computation.5 | async-start | bytes 1048576 | tf_op jit(solution)/shard_map/all_to_all | solution.py:62
  493.8 18.1 %all-to-all-start.5 = ((bf16[16,16,1024]{2,1,0:T(8,128)(2,1)}), bf16[16,16,1024]{2,1,0:T(8,128)(2,1)S(1)}, u32[]{:S(2)}, u32[]{:S(2)}) async-start(bf16[16,16,1024]{2,1,0:T(8,128)(2,1)} %bitcast.23), calls=%async_computation.8 | async-start | bytes 1048576 | tf_op jit(solution)/shard_map/all_to_all | solution.py:62
Sparse Core Ops, SparseCore 0:
  31.0 10.7 all-gather.3
  52.2 10.7 all-gather.5
  252.2 11.7 all-gather.7
  266.1 10.7 reduce-scatter.3
  439.5 14.2 reduce-scatter.5
  455.9 10.7 reduce-scatter.7
where the time goes:
time: 526 us; the launch traced here: 520 us
  waiting for transfers between devices  413 us (79%)
  starting transfers between devices  43.5 us (8%)
  matrix products  35.2 us (7%)
  between operations  14.3 us (3%)
  other arithmetic  9.92 us (2%)
    all_to_all x3, waiting for transfers between devices, shards(): lax.all_to_all(outgoing, 'expert', split_axis=0, concat_axis=0, tiled=True)  214 us
    ppermute x2, waiting for transfers between devices, shifted(): lax.ppermute(value, axis, [(i, (i + by) % devices) for i in range(devices)])  166 us
    all_to_all x3, waiting for transfers between devices, shards(): lax.all_to_all(served, 'expert', split_axis=0, concat_axis=0, tiled=True)  32.7 us
    dot_general x3, matrix products, apply_rows(): return jnp.dot(hidden, down_matrix, preferred_element_type=jnp.float32)  28.9 us
    all_to_all x3, starting transfers between devices, shards(): lax.all_to_all(served, 'expert', split_axis=0, concat_axis=0, tiled=True)  22.7 us
    all_to_all x3, starting transfers between devices, shards(): lax.all_to_all(outgoing, 'expert', split_axis=0, concat_axis=0, tiled=True)  18 us
  transfers between devices with their start and end apart: 14, of which 8 were waited for; matrix products, arithmetic and copies ran while one was open for 8% of the time, Pallas kernels for 0%

commit v1 on v0

v1 whole, which is shorter than its diff:
```python
import functools

import jax
import jax.numpy as jnp
from jax import lax
from jax.experimental import pallas as pl
from jax.experimental.pallas import tpu as pltpu
from jax.sharding import PartitionSpec as P

MESH = pl.DeviceIdType.MESH
PIECE = 512


def slots_of(language, placement, swap_flags, experts, capacity):
    labels = jnp.arange(experts, dtype=jnp.int32)
    resident = jnp.where(swap_flags == 1, (labels + experts // 2) % experts, labels)
    moved = jnp.sum(jnp.where(placement[:, :, None] == labels, resident, 0), axis=2)
    steps = jnp.arange(placement.shape[0], dtype=jnp.int32)[:, None]
    device_of = jnp.where(steps == 0, placement, moved)
    ids = language[:, :, 0]
    target = jnp.sum(jnp.where(ids[:, :, None] == labels, device_of[:, None, :], 0), axis=2)
    rows = jnp.arange(ids.shape[1], dtype=jnp.int32)
    earlier = (ids[:, :, None] == ids[:, None, :]) & (rows[None, :] < rows[:, None])
    return target * capacity + jnp.sum(earlier.astype(jnp.int32), axis=2)


def layer_kernel(
    slot_row, slot_col, states, up, down, out,
    up_all, down_all, outgoing, arrived, results, returned, total,
    own_sem, half_send, half_recv, go_send, go_recv, back_send, back_recv,
):
    steps, experts, capacity, width = outgoing.shape
    pieces = up_all.shape[0] // 2
    rows = states.shape[1]
    slots = experts * capacity
    core, me = lax.axis_index("dp"), lax.axis_index("expert")
    other = 1 - core

    def peer(k):
        return lax.rem(me + k, experts)

    def over_peers(body):
        def step_of(k, carry):
            body(peer(k))
            return carry
        lax.fori_loop(1, experts, step_of, 0)

    def own_copies(piece):
        columns = pl.ds(piece * PIECE, PIECE)
        return (
            pltpu.make_async_copy(up.at[:, columns], up_all.at[piece], own_sem.at[0, piece]),
            pltpu.make_async_copy(down.at[columns, :], down_all.at[piece], own_sem.at[1, piece]),
        )

    def half_copies(piece):
        columns = pl.ds(piece * PIECE, PIECE)
        ends = dict(device_id=(other, me), device_id_type=MESH)
        return (
            pltpu.make_async_remote_copy(
                up.at[:, columns], up_all.at[pieces + piece], half_send.at[0, piece], half_recv.at[0, piece], **ends),
            pltpu.make_async_remote_copy(
                down.at[columns, :], down_all.at[pieces + piece], half_send.at[1, piece], half_recv.at[1, piece], **ends),
        )

    def go_copy(step, device):
        return pltpu.make_async_remote_copy(
            outgoing.at[step, device], arrived.at[step, me], go_send.at[step, device], go_recv.at[step, me],
            device_id=(core, device), device_id_type=MESH)

    def go_arrival(step, device):
        return pltpu.make_async_remote_copy(
            outgoing.at[step, device], arrived.at[step, device], go_send.at[step, device], go_recv.at[step, device],
            device_id=(core, device), device_id_type=MESH)

    def back_copy(step, device):
        return pltpu.make_async_remote_copy(
            results.at[step, device], returned.at[step, me], back_send.at[step, device], back_recv.at[step, me],
            device_id=(core, device), device_id_type=MESH)

    def back_arrival(step, device):
        return pltpu.make_async_remote_copy(
            results.at[step, device], returned.at[step, device], back_send.at[step, device], back_recv.at[step, device],
            device_id=(core, device), device_id_type=MESH)

    for piece in range(pieces):
        for copy in own_copies(piece):
            copy.start()

    barrier = pltpu.get_barrier_semaphore()
    over_peers(lambda device: pl.semaphore_signal(
        barrier, inc=1, device_id=(core, device), device_id_type=MESH))
    pl.semaphore_signal(barrier, inc=1, device_id=(other, me), device_id_type=MESH)

    def fill(step):
        place = lax.broadcasted_iota(jnp.int32, (slots, rows), 0)
        pick = (place == slot_row[step]).astype(jnp.bfloat16)
        rows_out = jnp.dot(pick, states[step], preferred_element_type=jnp.float32)
        outgoing[step] = rows_out.astype(jnp.bfloat16).reshape(experts, capacity, width)

    fill(0)
    pl.semaphore_wait(barrier, experts)
    for step in range(steps):
        if step:
            fill(step)
        over_peers(lambda device: go_copy(step, device).start())
        if step == 0:
            for piece in range(pieces):
                for copy in half_copies(piece):
                    copy.start()
        arrived[step, me] = outgoing[step, me]

    def add_piece(step, piece, first):
        x = arrived[step].reshape(slots, width)
        hidden = jnp.dot(x, up_all[piece], preferred_element_type=jnp.float32)
        hidden = jnp.maximum(hidden, 0.0).astype(jnp.bfloat16)
        term = jnp.dot(hidden, down_all[piece], preferred_element_type=jnp.float32)
        if first:
            total[...] = term
        else:
            total[...] += term

    def combine(step):
        over_peers(lambda device: back_arrival(step, device).wait_recv())
        place = lax.broadcasted_iota(jnp.int32, (rows, slots), 1)
        pick = (place == slot_col[step]).astype(jnp.bfloat16)
        update = jnp.dot(
            pick, returned[step].reshape(slots, width), preferred_element_type=jnp.float32)
        out[step] = (states[step].astype(jnp.float32) + update).astype(jnp.bfloat16)

    for step in range(steps):
        over_peers(lambda device: go_arrival(step, device).wait_recv())
        for piece in range(2 * pieces):
            if step == 0:
                if piece < pieces:
                    for copy in own_copies(piece):
                        copy.wait()
                else:
                    for copy in half_copies(piece - pieces):
                        copy.wait_recv()
            add_piece(step, piece, piece == 0)
        results[step] = total[...].astype(jnp.bfloat16).reshape(experts, capacity, width)
        over_peers(lambda device: back_copy(step, device).start())
        returned[step, me] = results[step, me]
    for step in range(steps):
        combine(step)

    for piece in range(pieces):
        for copy in half_copies(piece):
            copy.wait_send()
    for step in range(steps):
        over_peers(lambda device: go_copy(step, device).wait_send())
        over_peers(lambda device: back_copy(step, device).wait_send())


def kernel_layer(states, slot_index, up_local, down_local, experts, capacity):
    steps, rows, width = states.shape
    pieces = up_local.shape[1] // PIECE
    blocks = pltpu.VMEM((steps, experts, capacity, width), jnp.bfloat16)
    sems = pltpu.SemaphoreType.DMA
    vmem = pl.BlockSpec(memory_space=pltpu.VMEM)
    anywhere = pl.BlockSpec(memory_space=pl.ANY)
    return pl.pallas_call(
        layer_kernel,
        out_shape=jax.ShapeDtypeStruct((steps, rows, width), jnp.bfloat16),
        in_specs=[vmem, vmem, vmem, anywhere, anywhere],
        out_specs=vmem,
        scratch_shapes=[
            pltpu.VMEM((2 * pieces, width, PIECE), jnp.bfloat16),
            pltpu.VMEM((2 * pieces, PIECE, width), jnp.bfloat16),
            blocks, blocks, blocks, blocks,
            pltpu.VMEM((experts * capacity, width), jnp.float32),
            sems((2, pieces)), sems((2, pieces)), sems((2, pieces)),
            sems((steps, experts)), sems((steps, experts)),
            sems((steps, experts)), sems((steps, experts)),
        ],
        compiler_params=pltpu.CompilerParams(
            collective_id=0, has_side_effects=True, vmem_limit_bytes=56 * 2**20),
        cost_estimate=pl.CostEstimate(
            flops=8 * steps * experts * capacity * width * up_local.shape[1],
            bytes_accessed=4 * up_local.size * 2, transcendentals=0),
    )(slot_index[:, None, :], slot_index[:, :, None], states, up_local, down_local)


def plain_layer(states, slot_index, up_local, down_local, experts, capacity):
    width = states.shape[2]
    slot_labels = jnp.arange(experts * capacity, dtype=jnp.int32)
    outputs = []
    for step in range(states.shape[0]):
        select = (slot_index[step][:, None] == slot_labels[None, :]).astype(jnp.bfloat16)
        outgoing = jnp.einsum("rs,rd->sd", select, states[step], preferred_element_type=jnp.float32)
        arrived = lax.all_to_all(
            outgoing.astype(jnp.bfloat16).reshape(experts, capacity, width),
            "expert", split_axis=0, concat_axis=0, tiled=True)
        both = lax.all_gather(
            arrived.reshape(experts * capacity, width), "dp", axis=0, tiled=True)
        hidden = jnp.maximum(jnp.dot(both, up_local, preferred_element_type=jnp.float32), 0.0)
        terms = jnp.dot(hidden.astype(jnp.bfloat16), down_local, preferred_element_type=jnp.float32)
        served = lax.psum_scatter(terms, "dp", scatter_dimension=0, tiled=True).astype(jnp.bfloat16)
        returned = lax.all_to_all(
            served.reshape(experts, capacity, width), "expert", split_axis=0, concat_axis=0, tiled=True)
        update = jnp.dot(
            select, returned.reshape(experts * capacity, width), preferred_element_type=jnp.float32)
        outputs.append((states[step].astype(jnp.float32) + update).astype(jnp.bfloat16))
    return jnp.stack(outputs)


def shards(states, language, placement, swap_flags, up_weight, down_weight):
    experts = lax.axis_size("expert")
    capacity = max(2, 2 * states.shape[1] // experts)
    slot_index = slots_of(language, placement, swap_flags, experts, capacity)
    layer = kernel_layer if capacity % 16 == 0 else plain_layer
    return layer(states, slot_index, up_weight[0], down_weight[0], experts, capacity)


def solution(mesh):
    rows_by = P(None, ("dp", "expert"), None)
    return jax.shard_map(
        shards,
        mesh=mesh,
        in_specs=(rows_by, rows_by, P(), P(), P("expert", None, "dp"), P("expert", "dp", None)),
        out_specs=rows_by,
        check_vma=False,
    )
```

time: 526 us -> 85.5 us (0.16); the launches traced: 520 us -> 85.2 us
  waiting for transfers between devices: 413 us -> 0 us
  Pallas kernels: 0 us -> 78.4 us
  starting transfers between devices: 43.5 us -> 0 us
  matrix products: 35.2 us -> 0 us
  between operations: 14.3 us -> 0.02 us
  other arithmetic: 9.92 us -> 2.65 us
    all_to_all x6 -> x0, waiting for transfers between devices: 246 us -> none  [the longest x3 214 us: shards(): lax.all_to_all(outgoing, 'expert', split_axis=0, concat_axis=0, tiled=True)]
    ppermute x2 -> x0, waiting for transfers between devices: 166 us -> none  [shifted(): lax.ppermute(value, axis, [(i, (i + by) % devices) for i in range(devices)])]
    pallas_call x0 -> x1, Pallas kernels: none -> 78.4 us  [kernel_layer(): pl.pallas_call(layer_kernel, out_shape=jax.ShapeDtypeStruct((steps, rows,...]
    all_to_all x6 -> x0, starting transfers between devices: 40.7 us -> none  [the longest x3 22.7 us: shards(): lax.all_to_all(served, 'expert', split_axis=0, concat_axis=0, tiled=True)]
    dot_general x9 -> x0, matrix products: 35.2 us -> none  [the longest x3 28.9 us: apply_rows(): return jnp.dot(hidden, down_matrix, preferred_element_type=jnp.float32)]
    convert_element_type x6 -> x0, other arithmetic: 6.9 us -> none  [the longest x3 6.63 us: expert_fn(): own_share.astype(jnp.bfloat16)]
  transfers between devices with their start and end apart: 14 -> 0, of which waited for: 8 -> 0; matrix products, arithmetic and copies ran while one was open for 8% -> 0% of each run, Pallas kernels for 0% -> 0%
where the time goes in v1:
time: 85.5 us; the launch traced here: 85.2 us
  Pallas kernels  78.4 us (92%)
  local copies, waits for them, and re-layouts  4.15 us (5%)
  other arithmetic  2.65 us (3%)
    pallas_call x1, Pallas kernels, kernel_layer(): pl.pallas_call(layer_kernel, out_shape=jax.ShapeDtypeStruct((steps, rows,...  78.4 us
    unnamed x2, local copies, waits for them, and re-layouts  2.74 us

profile of v1, /device:TPU:15, one launch (start us, length us, event | category | flops | bytes accessed | tf_op | source)
XLA Modules:
  0.0 85.2 jit_solution(2419723214822950341)
XLA Ops:
  0.0 0.7 compare_select_fusion.2
  0.7 0.9 %select_reduce_fusion.1 = s32[3,16]{1,0:T(4,128)S(1)} fusion(s32[16]{0:T(128)S(1)} %compare_select_fusion.2, s32[3,16]{1,0:T(4,128)} %param.8), kind=kLoop, calls=%fused_computation.3 | loop fusion | flops 2256 | bytes 448 | tf_op jit(solution)/shard_map/reduce_sum | solution.py:17
  1.6 0.8 broadcast_select_fusion
  2.3 0.7 copy.12
  3.0 0.1 select_reduce_fusion
  3.1 0.2 convert_reduce_fusion
  3.3 0.6 add.35.slot_row
  3.9 0.8 copy.9.slot_col
  4.8 78.4 %shard_map.64 = bf16[3,128,1024]{2,1,0:T(8,128)(2,1)} custom-call(s32[3,1,128]{2,1,0:T(1,128)} %add.35.slot_row, s32[3,128,1]{2,1,0:T(8,128)} %copy.9.slot_col, bf16[3,128,1024]{2,1,0:T(8,128)(2,1)} %states.1, bf16[1024,2048]{1,0:T(8,128)(2,1)} %bitcast.9, bf16[2048,1024]{1,0:T(8,128)(2,1)} %bitcast.10), custom_call_target="tpu_custom_call" | custom-call | flops 12884901888 | bytes 16777216 | tf_op jit(solution)/shard_map/pallas_call | solution.py:162
  83.2 2.1 %copy.14 = bf16[3,128,1024]{2,1,0:T(8,128)(2,1)} copy(bf16[3,128,1024]{2,1,0:T(8,128)(2,1)} %shard_map.64) | data formatting | bytes 1572864
  (3 shorter events, 0.0 us)

commit v2 on v1

--- a/solution.py
+++ b/solution.py
@@ -1,5 +1,3 @@
-import functools
-
 import jax
 import jax.numpy as jnp
 from jax import lax
@@ -25,8 +23,8 @@
 
 
 def layer_kernel(
-    slot_row, slot_col, states, up, down, out,
-    up_all, down_all, outgoing, arrived, results, returned, total,
+    language, placement, swap_flags, states, up, down, out,
+    up_all, down_all, outgoing, arrived, results, returned, picks, total,
     own_sem, half_send, half_recv, go_send, go_recv, back_send, back_recv,
 ):
     steps, experts, capacity, width = outgoing.shape
@@ -82,18 +80,33 @@
             results.at[step, device], returned.at[step, device], back_send.at[step, device], back_recv.at[step, device],
             device_id=(core, device), device_id_type=MESH)
 
-    for piece in range(pieces):
-        for copy in own_copies(piece):
-            copy.start()
-
     barrier = pltpu.get_barrier_semaphore()
     over_peers(lambda device: pl.semaphore_signal(
         barrier, inc=1, device_id=(core, device), device_id_type=MESH))
     pl.semaphore_signal(barrier, inc=1, device_id=(other, me), device_id_type=MESH)
 
     def fill(step):
+        langs = placement.shape[1]
+        label = lax.broadcasted_iota(jnp.int32, (langs, langs), 0)
+        along = lax.broadcasted_iota(jnp.int32, (langs, langs), 1)
+        served_by = placement[pl.ds(step, 1), :].astype(jnp.float32)
+        target = jnp.sum(jnp.where(label == along, served_by, 0.0), axis=1, keepdims=True)
+        if step:
+            flags = swap_flags[...].astype(jnp.float32)
+            flag = jnp.sum(
+                jnp.where(along.astype(jnp.float32) == target, flags, 0.0), axis=1, keepdims=True)
+            half = experts // 2
+            traded = jnp.where(target < half, target + half, target - half)
+            target = jnp.where(flag > 0.5, traded, target)
+        hot = lax.broadcasted_iota(jnp.int32, (langs, rows), 0) == language[step]
+        before = (lax.broadcasted_iota(jnp.int32, (rows, rows), 0)
+                  < lax.broadcasted_iota(jnp.int32, (rows, rows), 1))
+        earlier = jnp.dot(
+            hot.astype(jnp.bfloat16), before.astype(jnp.bfloat16), preferred_element_type=jnp.float32)
+        slot = jnp.sum(jnp.where(hot, target * capacity + earlier, 0.0), axis=0, keepdims=True)
         place = lax.broadcasted_iota(jnp.int32, (slots, rows), 0)
-        pick = (place == slot_row[step]).astype(jnp.bfloat16)
+        pick = (place == slot.astype(jnp.int32)).astype(jnp.bfloat16)
+        picks[step] = pick
         rows_out = jnp.dot(pick, states[step], preferred_element_type=jnp.float32)
         outgoing[step] = rows_out.astype(jnp.bfloat16).reshape(experts, capacity, width)
 
@@ -105,7 +118,7 @@
         over_peers(lambda device: go_copy(step, device).start())
         if step == 0:
             for piece in range(pieces):
-                for copy in half_copies(piece):
+                for copy in own_copies(piece) + half_copies(piece):
                     copy.start()
         arrived[step, me] = outgoing[step, me]
 
@@ -121,11 +134,10 @@
 
     def combine(step):
         over_peers(lambda device: back_arrival(step, device).wait_recv())
-        place = lax.broadcasted_iota(jnp.int32, (rows, slots), 1)
-        pick = (place == slot_col[step]).astype(jnp.bfloat16)
-        update = jnp.dot(
-            pick, returned[step].reshape(slots, width), preferred_element_type=jnp.float32)
-        out[step] = (states[step].astype(jnp.float32) + update).astype(jnp.bfloat16)
+        update = lax.dot_general(
+            picks[step], returned[step].reshape(slots, width), (((0,), (0,)), ((), ())),
+            preferred_element_type=jnp.float32)
+        out[step] = update.astype(jnp.bfloat16)
 
     for step in range(steps):
         over_peers(lambda device: go_arrival(step, device).wait_recv())
@@ -152,22 +164,23 @@
         over_peers(lambda device: back_copy(step, device).wait_send())
 
 
-def kernel_layer(states, slot_index, up_local, down_local, experts, capacity):
+def kernel_layer(states, language, placement, swap_flags, up_local, down_local, experts, capacity):
     steps, rows, width = states.shape
     pieces = up_local.shape[1] // PIECE
     blocks = pltpu.VMEM((steps, experts, capacity, width), jnp.bfloat16)
     sems = pltpu.SemaphoreType.DMA
     vmem = pl.BlockSpec(memory_space=pltpu.VMEM)
     anywhere = pl.BlockSpec(memory_space=pl.ANY)
-    return pl.pallas_call(
+    update = pl.pallas_call(
         layer_kernel,
         out_shape=jax.ShapeDtypeStruct((steps, rows, width), jnp.bfloat16),
-        in_specs=[vmem, vmem, vmem, anywhere, anywhere],
+        in_specs=[vmem, vmem, vmem, vmem, anywhere, anywhere],
         out_specs=vmem,
         scratch_shapes=[
             pltpu.VMEM((2 * pieces, width, PIECE), jnp.bfloat16),
             pltpu.VMEM((2 * pieces, PIECE, width), jnp.bfloat16),
             blocks, blocks, blocks, blocks,
+            pltpu.VMEM((steps, experts * capacity, rows), jnp.bfloat16),
             pltpu.VMEM((experts * capacity, width), jnp.float32),
             sems((2, pieces)), sems((2, pieces)), sems((2, pieces)),
             sems((steps, experts)), sems((steps, experts)),
@@ -178,10 +191,12 @@
         cost_estimate=pl.CostEstimate(
             flops=8 * steps * experts * capacity * width * up_local.shape[1],
             bytes_accessed=4 * up_local.size * 2, transcendentals=0),
-    )(slot_index[:, None, :], slot_index[:, :, None], states, up_local, down_local)
-
-
-def plain_layer(states, slot_index, up_local, down_local, experts, capacity):
+    )(language.reshape(steps, 1, rows), placement, swap_flags[None, :], states, up_local, down_local)
+    return (states.astype(jnp.float32) + update.astype(jnp.float32)).astype(jnp.bfloat16)
+
+
+def plain_layer(states, language, placement, swap_flags, up_local, down_local, experts, capacity):
+    slot_index = slots_of(language, placement, swap_flags, experts, capacity)
     width = states.shape[2]
     slot_labels = jnp.arange(experts * capacity, dtype=jnp.int32)
     outputs = []
@@ -207,9 +222,8 @@
 def shards(states, language, placement, swap_flags, up_weight, down_weight):
     experts = lax.axis_size("expert")
     capacity = max(2, 2 * states.shape[1] // experts)
-    slot_index = slots_of(language, placement, swap_flags, experts, capacity)
     layer = kernel_layer if capacity % 16 == 0 else plain_layer
-    return layer(states, slot_index, up_weight[0], down_weight[0], experts, capacity)
+    return layer(states, language, placement, swap_flags, up_weight[0], down_weight[0], experts, capacity)
 
 
 def solution(mesh):

time: 85.5 us -> 81 us (0.947)
  local copies, waits for them, and re-layouts: 4.15 us -> 0.01 us
    unnamed x2, local copies, waits for them, and re-layouts: 2.74 us -> 0.01 us
    convert_element_type x0 -> x1, other arithmetic: none -> 2.33 us  [kernel_layer(): (states.astype(jnp.float32) + update.astype(jnp.float32)).astype(jnp.bflo...]
    select_n x2 -> x0, other arithmetic: 1.42 us -> none  [the longest x1 0.76 us: slots_of(): device_of = jnp.where(steps == 0, placement, moved)]
    add x2 -> x0, local copies, waits for them, and re-layouts: 1.41 us -> none  [slots_of(): return target * capacity + jnp.sum(earlier.astype(jnp.int32), axis=2)]
    reduce_sum x3 -> x0, other arithmetic: 1.2 us -> none  [the longest x1 0.89 us: slots_of(): jnp.sum(jnp.where(placement[:, :, None] == labels, resident, 0), axis=2)]
where the time goes in v2:
time: 81 us; the launch traced here: 80.8 us
  Pallas kernels  78.4 us (97%)
  other arithmetic  2.33 us (3%)
    pallas_call x1, Pallas kernels, kernel_layer(): pl.pallas_call(layer_kernel, out_shape=jax.ShapeDtypeStruct((steps, rows,...  78.4 us
    convert_element_type x1, other arithmetic, kernel_layer(): (states.astype(jnp.float32) + update.astype(jnp.float32)).astype(jnp.bflo...  2.33 us

profile of v2, /device:TPU:15, one launch (start us, length us, event | category | flops | bytes accessed | tf_op | source)
XLA Modules:
  0.0 80.8 jit_solution(111615842869741030)
XLA Ops:
  0.0 0.0 copy-start
  0.0 78.4 %shard_map.64 = bf16[3,128,1024]{2,1,0:T(8,128)(2,1)} custom-call(s32[3,1,128]{2,1,0:T(1,128)} %bitcast.6, s32[3,16]{1,0:T(4,128)} %placement.1, s32[1,16]{1,0:T(1,128)} %bitcast.7, bf16[3,128,1024]{2,1,0:T(8,128)(2,1)} %states.1, bf16[1024,2048]{1,0:T(8,128)(2,1)} %bitcast.4, bf16[2048,1024]{1,0:T(8,128)(2,1)} %bitcast.5), custom_call_target="tpu_custom_call" | custom-call | flops 12884901888 | bytes 16777216 | tf_op jit(solution)/shard_map/pallas_call | solution.py:174
  78.4 0.0 copy-done
  78.5 2.3 %add_convert_fusion = bf16[3,128,1024]{2,1,0:T(8,128)(2,1)} fusion(bf16[3,128,1024]{2,1,0:T(8,128)(2,1)} %shard_map.64, bf16[3,128,1024]{2,1,0:T(8,128)(2,1)S(1)} %copy-done), kind=kLoop, calls=%fused_computation | loop fusion | flops 1572864 | bytes 2359296 | tf_op jit(solution)/shard_map/convert_element_type | solution.py:195
Async XLA Ops:
  0.0 78.4 %copy-start = (bf16[3,128,1024]{2,1,0:T(8,128)(2,1)S(1)}, bf16[3,128,1024]{2,1,0:T(8,128)(2,1)}, u32[]{:S(2)}) copy-start(bf16[3,128,1024]{2,1,0:T(8,128)(2,1)} %states.1) | copy-start | bytes 2359300

commit v3 on v2

--- a/solution.py
+++ b/solution.py
@@ -34,14 +34,21 @@
     core, me = lax.axis_index("dp"), lax.axis_index("expert")
     other = 1 - core
 
-    def peer(k):
-        return lax.rem(me + k, experts)
+    def peer(turn):
+        if experts & (experts - 1):
+            return lax.rem(me + turn + 1, experts)
+        offset = (1 - lax.rem(turn, 2)) * (experts // 2) + lax.div(turn + 1, 2)
+        device, bit = 0, 1
+        while bit < experts:
+            device += lax.rem(lax.div(me, bit) + lax.div(offset, bit), 2) * bit
+            bit *= 2
+        return device
 
     def over_peers(body):
-        def step_of(k, carry):
-            body(peer(k))
+        def step_of(turn, carry):
+            body(peer(turn))
             return carry
-        lax.fori_loop(1, experts, step_of, 0)
+        lax.fori_loop(0, experts - 1, step_of, 0)
 
     def own_copies(piece):
         columns = pl.ds(piece * PIECE, PIECE)

time: 81 us -> 82.2 us (1.015)
  Pallas kernels: 78.4 us -> 79.6 us
    pallas_call x1, Pallas kernels: 78.4 us -> 79.6 us  [kernel_layer(): pl.pallas_call(layer_kernel, out_shape=jax.ShapeDtypeStruct((steps, rows,...]
where the time goes in v3:
time: 82.2 us; the launch traced here: 81.9 us
  Pallas kernels  79.6 us (97%)
  other arithmetic  2.33 us (3%)
    pallas_call x1, Pallas kernels, kernel_layer(): pl.pallas_call(layer_kernel, out_shape=jax.ShapeDtypeStruct((steps, rows,...  79.6 us
    convert_element_type x1, other arithmetic, kernel_layer(): (states.astype(jnp.float32) + update.astype(jnp.float32)).astype(jnp.bflo...  2.33 us

profile of v3, /device:TPU:15, one launch (start us, length us, event | category | flops | bytes accessed | tf_op | source)
XLA Modules:
  0.0 81.9 jit_solution(12218848004120555168)
XLA Ops:
  0.0 0.0 copy-start
  0.0 79.6 %shard_map.64 = bf16[3,128,1024]{2,1,0:T(8,128)(2,1)} custom-call(s32[3,1,128]{2,1,0:T(1,128)} %bitcast.6, s32[3,16]{1,0:T(4,128)} %placement.1, s32[1,16]{1,0:T(1,128)} %bitcast.7, bf16[3,128,1024]{2,1,0:T(8,128)(2,1)} %states.1, bf16[1024,2048]{1,0:T(8,128)(2,1)} %bitcast.4, bf16[2048,1024]{1,0:T(8,128)(2,1)} %bitcast.5), custom_call_target="tpu_custom_call" | custom-call | flops 12884901888 | bytes 16777216 | tf_op jit(solution)/shard_map/pallas_call | solution.py:181
  79.6 0.0 copy-done
  79.6 2.3 %add_convert_fusion = bf16[3,128,1024]{2,1,0:T(8,128)(2,1)} fusion(bf16[3,128,1024]{2,1,0:T(8,128)(2,1)} %shard_map.64, bf16[3,128,1024]{2,1,0:T(8,128)(2,1)S(1)} %copy-done), kind=kLoop, calls=%fused_computation | loop fusion | flops 1572864 | bytes 2359296 | tf_op jit(solution)/shard_map/convert_element_type | solution.py:202
Async XLA Ops:
  0.0 79.6 %copy-start = (bf16[3,128,1024]{2,1,0:T(8,128)(2,1)S(1)}, bf16[3,128,1024]{2,1,0:T(8,128)(2,1)}, u32[]{:S(2)}) copy-start(bf16[3,128,1024]{2,1,0:T(8,128)(2,1)} %states.1) | copy-start | bytes 2359300

commit v4 on v2

--- a/solution.py
+++ b/solution.py
@@ -110,17 +110,20 @@
         rows_out = jnp.dot(pick, states[step], preferred_element_type=jnp.float32)
         outgoing[step] = rows_out.astype(jnp.bfloat16).reshape(experts, capacity, width)
 
+    def send(step):
+        over_peers(lambda device: go_copy(step, device).start())
+        arrived[step, me] = outgoing[step, me]
+
     fill(0)
     pl.semaphore_wait(barrier, experts)
-    for step in range(steps):
-        if step:
-            fill(step)
-        over_peers(lambda device: go_copy(step, device).start())
-        if step == 0:
-            for piece in range(pieces):
-                for copy in own_copies(piece) + half_copies(piece):
-                    copy.start()
-        arrived[step, me] = outgoing[step, me]
+    send(0)
+    for piece in range(pieces):
+        for copy in own_copies(piece) + half_copies(piece):
+            copy.start()
+    for step in range(1, steps):
+        fill(step)
+        if step == 1:
+            send(step)
 
     def add_piece(step, piece, first):
         x = arrived[step].reshape(slots, width)
@@ -141,6 +144,8 @@
 
     for step in range(steps):
         over_peers(lambda device: go_arrival(step, device).wait_recv())
+        if step + 2 < steps:
+            send(step + 2)
         for piece in range(2 * pieces):
             if step == 0:
                 if piece < pieces:
@@ -173,7 +178,7 @@
     anywhere = pl.BlockSpec(memory_space=pl.ANY)
     update = pl.pallas_call(
         layer_kernel,
-        out_shape=jax.ShapeDtypeStruct((steps, rows, width), jnp.bfloat16),
+        out_shape=pltpu.VMEM((steps, rows, width), jnp.bfloat16),
         in_specs=[vmem, vmem, vmem, vmem, anywhere, anywhere],
         out_specs=vmem,
         scratch_shapes=[

time: 81 us -> 78.9 us (0.974)
  other arithmetic: 2.33 us -> 1.19 us
  Pallas kernels: 78.4 us -> 77.5 us
    convert_element_type x1, other arithmetic: 2.33 us -> 1.19 us  [kernel_layer(): (states.astype(jnp.float32) + update.astype(jnp.float32)).astype(jnp.bflo...]
    pallas_call x1, Pallas kernels: 78.4 us -> 77.5 us  [kernel_layer(): pl.pallas_call(layer_kernel, out_shape=pltpu.VMEM((steps, rows, width), j...]
where the time goes in v4:
time: 78.9 us; the launch traced here: 78.8 us
  Pallas kernels  77.5 us (98%)
  other arithmetic  1.19 us (2%)
    pallas_call x1, Pallas kernels, kernel_layer(): pl.pallas_call(layer_kernel, out_shape=pltpu.VMEM((steps, rows, width), j...  77.5 us

profile of v4, /device:TPU:15, one launch (start us, length us, event | category | flops | bytes accessed | tf_op | source)
XLA Modules:
  0.0 78.8 jit_solution(5605242728826442354)
XLA Ops:
  0.0 0.0 copy-start
  0.0 77.5 %shard_map.64 = bf16[3,128,1024]{2,1,0:T(8,128)(2,1)S(1)} custom-call(s32[3,1,128]{2,1,0:T(1,128)} %bitcast.6, s32[3,16]{1,0:T(4,128)} %placement.1, s32[1,16]{1,0:T(1,128)} %bitcast.7, bf16[3,128,1024]{2,1,0:T(8,128)(2,1)} %states.1, bf16[1024,2048]{1,0:T(8,128)(2,1)} %bitcast.4, bf16[2048,1024]{1,0:T(8,128)(2,1)} %bitcast.5), custom_call_target="tpu_custom_call" | custom-call | flops 12884901888 | bytes 16777216 | tf_op jit(solution)/shard_map/pallas_call | solution.py:179
  77.6 0.0 copy-done
  77.6 1.2 %add_convert_fusion = bf16[3,128,1024]{2,1,0:T(8,128)(2,1)} fusion(bf16[3,128,1024]{2,1,0:T(8,128)(2,1)S(1)} %shard_map.64, bf16[3,128,1024]{2,1,0:T(8,128)(2,1)S(1)} %copy-done), kind=kLoop, calls=%fused_computation | loop fusion | flops 1572864 | bytes 2359296 | tf_op jit(solution)/shard_map/convert_element_type | solution.py:200
Async XLA Ops:
  0.0 77.6 %copy-start = (bf16[3,128,1024]{2,1,0:T(8,128)(2,1)S(1)}, bf16[3,128,1024]{2,1,0:T(8,128)(2,1)}, u32[]{:S(2)}) copy-start(bf16[3,128,1024]{2,1,0:T(8,128)(2,1)} %states.1) | copy-start | bytes 2359300

commit v5 on v4

--- a/solution.py
+++ b/solution.py
@@ -23,9 +23,9 @@
 
 
 def layer_kernel(
-    language, placement, swap_flags, states, up, down, out,
-    up_all, down_all, outgoing, arrived, results, returned, picks, total,
-    own_sem, half_send, half_recv, go_send, go_recv, back_send, back_recv,
+    language, placement, swap_flags, states_in, up, down, out,
+    up_all, down_all, outgoing, arrived, results, returned, picks, total, states,
+    state_sem, own_sem, half_send, half_recv, go_send, go_recv, back_send, back_recv,
 ):
     steps, experts, capacity, width = outgoing.shape
     pieces = up_all.shape[0] // 2
@@ -36,6 +36,15 @@
 
     def peer(k):
         return lax.rem(me + k, experts)
+
+    def send_over_peers(body):
+        if experts & (experts - 1):
+            return over_peers(body)
+        bits = [1 << place for place in range(experts.bit_length() - 1)]
+        flips = [bit - 2 * bit * lax.rem(lax.div(me, bit), 2) for bit in bits]
+        for turn in range(experts - 1):
+            offset = (turn + 1) // 2 + (0 if turn % 2 else experts // 2)
+            body(me + sum(flip for bit, flip in zip(bits, flips) if offset & bit))
 
     def over_peers(body):
         def step_of(k, carry):
@@ -80,6 +89,11 @@
             results.at[step, device], returned.at[step, device], back_send.at[step, device], back_recv.at[step, device],
             device_id=(core, device), device_id_type=MESH)
 
+    def state_copy(step):
+        return pltpu.make_async_copy(states_in.at[step], states.at[step], state_sem.at[step])
+
+    for step in range(steps):
+        state_copy(step).start()
     barrier = pltpu.get_barrier_semaphore()
     over_peers(lambda device: pl.semaphore_signal(
         barrier, inc=1, device_id=(core, device), device_id_type=MESH))
@@ -107,11 +121,12 @@
         place = lax.broadcasted_iota(jnp.int32, (slots, rows), 0)
         pick = (place == slot.astype(jnp.int32)).astype(jnp.bfloat16)
         picks[step] = pick
+        state_copy(step).wait()
         rows_out = jnp.dot(pick, states[step], preferred_element_type=jnp.float32)
         outgoing[step] = rows_out.astype(jnp.bfloat16).reshape(experts, capacity, width)
 
     def send(step):
-        over_peers(lambda device: go_copy(step, device).start())
+        send_over_peers(lambda device: go_copy(step, device).start())
         arrived[step, me] = outgoing[step, me]
 
     fill(0)
@@ -156,7 +171,7 @@
                         copy.wait_recv()
             add_piece(step, piece, piece == 0)
         results[step] = total[...].astype(jnp.bfloat16).reshape(experts, capacity, width)
-        over_peers(lambda device: back_copy(step, device).start())
+        send_over_peers(lambda device: back_copy(step, device).start())
         returned[step, me] = results[step, me]
     for step in range(steps):
         combine(step)
@@ -179,7 +194,7 @@
     update = pl.pallas_call(
         layer_kernel,
         out_shape=pltpu.VMEM((steps, rows, width), jnp.bfloat16),
-        in_specs=[vmem, vmem, vmem, vmem, anywhere, anywhere],
+        in_specs=[vmem, vmem, vmem, anywhere, anywhere, anywhere],
         out_specs=vmem,
         scratch_shapes=[
             pltpu.VMEM((2 * pieces, width, PIECE), jnp.bfloat16),
@@ -187,7 +202,8 @@
             blocks, blocks, blocks, blocks,
             pltpu.VMEM((steps, experts * capacity, rows), jnp.bfloat16),
             pltpu.VMEM((experts * capacity, width), jnp.float32),
-            sems((2, pieces)), sems((2, pieces)), sems((2, pieces)),
+            pltpu.VMEM(states.shape, states.dtype),
+            sems((steps,)), sems((2, pieces)), sems((2, pieces)), sems((2, pieces)),
             sems((steps, experts)), sems((steps, experts)),
             sems((steps, experts)), sems((steps, experts)),
         ],

time: 78.9 us -> 79.2 us (level)
  no operation moved by 1% of the time
where the time goes in v5:
time: 79.2 us; the launch traced here: 78.6 us
  Pallas kernels  77.4 us (98%)
  other arithmetic  1.19 us (2%)
    pallas_call x1, Pallas kernels, kernel_layer(): pl.pallas_call(layer_kernel, out_shape=pltpu.VMEM((steps, rows, width), j...  77.4 us

profile of v5, /device:TPU:15, one launch (start us, length us, event | category | flops | bytes accessed | tf_op | source)
XLA Modules:
  0.0 78.6 jit_solution(9635900753873781344)
XLA Ops:
  0.0 0.0 copy-start
  0.0 77.4 %shard_map.64 = bf16[3,128,1024]{2,1,0:T(8,128)(2,1)S(1)} custom-call(s32[3,1,128]{2,1,0:T(1,128)} %bitcast.6, s32[3,16]{1,0:T(4,128)} %placement.1, s32[1,16]{1,0:T(1,128)} %bitcast.7, bf16[3,128,1024]{2,1,0:T(8,128)(2,1)} %states_in.1, bf16[1024,2048]{1,0:T(8,128)(2,1)} %bitcast.4, bf16[2048,1024]{1,0:T(8,128)(2,1)} %bitcast.5), custom_call_target="tpu_custom_call" | custom-call | flops 12884901888 | bytes 16777216 | tf_op jit(solution)/shard_map/pallas_call | solution.py:194
  77.4 0.0 copy-done
  77.4 1.2 %add_convert_fusion = bf16[3,128,1024]{2,1,0:T(8,128)(2,1)} fusion(bf16[3,128,1024]{2,1,0:T(8,128)(2,1)S(1)} %shard_map.64, bf16[3,128,1024]{2,1,0:T(8,128)(2,1)S(1)} %copy-done), kind=kLoop, calls=%fused_computation | loop fusion | flops 1572864 | bytes 2359296 | tf_op jit(solution)/shard_map/convert_element_type | solution.py:216
Async XLA Ops:
  0.0 77.4 %copy-start = (bf16[3,128,1024]{2,1,0:T(8,128)(2,1)S(1)}, bf16[3,128,1024]{2,1,0:T(8,128)(2,1)}, u32[]{:S(2)}) copy-start(bf16[3,128,1024]{2,1,0:T(8,128)(2,1)} %states_in.1) | copy-start | bytes 2359300

commit v6 on v4

--- a/solution.py
+++ b/solution.py
@@ -35,7 +35,7 @@
     other = 1 - core
 
     def peer(k):
-        return lax.rem(me + k, experts)
+        return lax.rem(me + k + core * (experts - 2 * k), experts)
 
     def over_peers(body):
         def step_of(k, carry):

time: 78.9 us -> 79.6 us (level)
  the two profiles are of different devices: /device:TPU:15 before, /device:TPU:1 now
where the time goes in v6:
time: 79.6 us; the launch traced here: 79.5 us
  Pallas kernels  78.3 us (98%)
  other arithmetic  1.19 us (1%)
    pallas_call x1, Pallas kernels, kernel_layer(): pl.pallas_call(layer_kernel, out_shape=pltpu.VMEM((steps, rows, width), j...  78.3 us

profile of v6, /device:TPU:1, one launch (start us, length us, event | category | flops | bytes accessed | tf_op | source)
XLA Modules:
  0.0 79.5 jit_solution(4196558818346041676)
XLA Ops:
  0.0 0.0 copy-start
  0.0 78.3 %shard_map.64 = bf16[3,128,1024]{2,1,0:T(8,128)(2,1)S(1)} custom-call(s32[3,1,128]{2,1,0:T(1,128)} %bitcast.6, s32[3,16]{1,0:T(4,128)} %placement.1, s32[1,16]{1,0:T(1,128)} %bitcast.7, bf16[3,128,1024]{2,1,0:T(8,128)(2,1)} %states.1, bf16[1024,2048]{1,0:T(8,128)(2,1)} %bitcast.4, bf16[2048,1024]{1,0:T(8,128)(2,1)} %bitcast.5), custom_call_target="tpu_custom_call" | custom-call | flops 12884901888 | bytes 16777216 | tf_op jit(solution)/shard_map/pallas_call | solution.py:179
  78.3 0.0 copy-done
  78.3 1.2 %add_convert_fusion = bf16[3,128,1024]{2,1,0:T(8,128)(2,1)} fusion(bf16[3,128,1024]{2,1,0:T(8,128)(2,1)S(1)} %shard_map.64, bf16[3,128,1024]{2,1,0:T(8,128)(2,1)S(1)} %copy-done), kind=kLoop, calls=%fused_computation | loop fusion | flops 1572864 | bytes 2359296 | tf_op jit(solution)/shard_map/convert_element_type | solution.py:200
Async XLA Ops:
  0.0 78.3 %copy-start = (bf16[3,128,1024]{2,1,0:T(8,128)(2,1)S(1)}, bf16[3,128,1024]{2,1,0:T(8,128)(2,1)}, u32[]{:S(2)}) copy-start(bf16[3,128,1024]{2,1,0:T(8,128)(2,1)} %states.1) | copy-start | bytes 2359300
